TPU v7x, 32 devices: a whole 2x2x4 slice. The times are simulated.
32 devices in a mesh: segment: 2 (over y), fsdp: 4 (over x, core), seq: 4 (over z).
Axes of the slice: x: 2, y: 2, z: 4, core: 2. Of those that a mesh axis runs over, the one named last changes fastest.
Arguments:
- arriving: bfloat16 [2, 4, 768, 2048], P('segment', 'fsdp', 'seq'), may hold values from -6 to 6
- gain: float32 [2, 2048], P('segment'), may hold values from 0.1 to 1.9
- input_weight: bfloat16 [2, 2048, 16, 3, 128], P('segment', 'fsdp', 'seq')
- output_weight: bfloat16 [2, 16, 128, 2048], P('segment', 'seq', None, 'fsdp'), may hold values from -1 to 1
- block_pattern: int32 [2, 4, 24, 6], P('segment', 'fsdp'), may hold values from 0 to 23, as said below
Outputs:
- passed: bfloat16 [2, 4, 768, 2048], P('segment', 'fsdp', 'seq')
Inputs may be any that keep to these rules, and one draw needn't show every extreme that they name: `block_pattern`: row j of a document lists 6 different blocks; the first three are j - 1, j and j + 1 modulo 24, and block 0 is listed in every row.
All inputs are finite; a program needn't handle non-finite values.
Results may differ from a plain program's by a relative error of at most 0.012.
Values may be sent and summed in bfloat16 or wider, within the bound.
A program may use at most 64 MiB of HBM per device.

v0:
```python
import jax
import jax.numpy as jnp
from jax import lax
from jax.sharding import PartitionSpec as P

BLOCK = 32
SEL = 6
EPSILON = 1e-05


def passed_along(value, axis, steps):
    count = lax.axis_size(axis)
    pairs = [(source, (source + steps) % count) for source in range(count)]
    return lax.ppermute(value, axis, pairs)


def normalize(tokens, gain_row):
    values = tokens.astype(jnp.float32)
    spread = jnp.mean(values * values, axis=-1, keepdims=True)
    return (values * lax.rsqrt(spread + EPSILON) * gain_row).astype(jnp.bfloat16)


def attend(projected, pattern_rows):
    length, head_group, triple, head_width = projected.shape
    block_count = length // BLOCK
    query_rows = projected[:, :, 0].reshape(block_count, BLOCK, head_group, head_width)
    key_blocks = projected[:, :, 1].reshape(block_count, BLOCK, head_group, head_width)
    value_blocks = projected[:, :, 2].reshape(block_count, BLOCK, head_group, head_width)
    key_rows = jnp.take(key_blocks, pattern_rows, axis=0).reshape(
        block_count, SEL * BLOCK, head_group, head_width
    )
    value_rows = jnp.take(value_blocks, pattern_rows, axis=0).reshape(
        block_count, SEL * BLOCK, head_group, head_width
    )
    scores = jnp.einsum(
        "qbge,qnge->gqbn", query_rows, key_rows, preferred_element_type=jnp.float32
    ) * head_width ** (-0.5)
    row_max = jnp.max(scores, axis=-1, keepdims=True)
    exponent = jnp.exp(scores - row_max)
    weights = (exponent / jnp.sum(exponent, axis=-1, keepdims=True)).astype(jnp.bfloat16)
    mixed_rows = jnp.einsum(
        "gqbn,qnge->qbge", weights, value_rows, preferred_element_type=jnp.float32
    )
    return mixed_rows.astype(jnp.bfloat16).reshape(length, head_group * head_width)


def body(arriving, gain, input_weight, output_weight, block_pattern):
    tokens = arriving[0, 0]
    row_count = tokens.shape[0]
    normed = normalize(tokens, gain[0])
    slab_rows, head_group, triple, head_size = input_weight.shape[1:]
    columns = head_group * triple * head_size
    panel_flat = input_weight[0].reshape(slab_rows, columns)
    length = row_count * lax.axis_size("seq")
    whole_panel = lax.all_gather(panel_flat, "fsdp", axis=0, tiled=True)
    projected = jnp.dot(
        lax.all_gather(normed, "seq", axis=0, tiled=True),
        whole_panel,
        preferred_element_type=jnp.float32,
    )
    projected = projected.astype(jnp.bfloat16).reshape(length, head_group, triple, head_size)
    mixed_rows = attend(projected, block_pattern[0, 0])
    out_panel = output_weight[0].reshape(head_group * head_size, -1)
    whole_out = lax.all_gather(out_panel, "fsdp", axis=1, tiled=True)
    branch = lax.psum_scatter(
        jnp.dot(mixed_rows, whole_out, preferred_element_type=jnp.float32).astype(jnp.bfloat16),
        "seq",
        scatter_dimension=0,
        tiled=True,
    ).astype(jnp.float32)
    updated = (tokens.astype(jnp.float32) + branch).astype(jnp.bfloat16)
    passed = passed_along(updated, "segment", 1)
    return passed[None, None]


def solution(mesh):
    in_specs = (
        P("segment", "fsdp", "seq", None),
        P("segment", None),
        P("segment", "fsdp", "seq", None, None),
        P("segment", "seq", None, "fsdp"),
        P("segment", "fsdp", None, None),
    )
    out_specs = P("segment", "fsdp", "seq", None)
    return jax.shard_map(body, mesh=mesh, in_specs=in_specs, out_specs=out_specs, check_vma=False)
```

profile of v0, /device:TPU:0, one launch (start us, length us, event | category | flops | bytes accessed | tf_op | source)
XLA Modules:
  0.0 277.0 jit_solution(2608817675597869169)
XLA Ops:
  6.5 0.0 copy-start.1
  6.5 0.0 all-gather.4.cloned.1.call-start
  6.5 1.5 fusion.4
  8.0 2.3 fusion.6
  10.3 0.0 copy-start.2
  10.3 0.0 all-gather.4.cloned.1.call-update
  10.3 0.0 all-gather.6.cloned.1.call-start
  10.4 0.0 copy-done.1
  10.4 2.6 copy.24
  13.0 0.0 all-gather.6.cloned.1.call-update
  13.0 0.0 all-gather.8.cloned.1.call-start
  13.0 0.7 all-gather.8.cloned.1.call-update
  13.7 0.0 reduce-scatter.2.cloned.1.call-start
  13.8 0.0 copy-done.2
  13.8 0.1 copy.27
  13.9 0.1 reshape.54
  14.0 0.1 copy.23
  14.1 62.6 %all-gather.4.cloned.1.call-done = bf16[768,2048]{1,0:T(8,128)(2,1)} async-done(((bf16[192,2048]{1,0:T(8,128)(2,1)}), bf16[768,2048]{1,0:T(8,128)(2,1)}) %all-gather.4.cloned.1.call-update) | async-done | bytes 3145744 | tf_op jit(solution)/shard_map/all_gather | solution.py:57
  76.7 46.6 %all-gather.6.cloned.1.call-done = bf16[2048,1536]{0,1:T(8,128)(2,1)} async-done(((bf16[512,1536]{0,1:T(8,128)(2,1)}), bf16[2048,1536]{0,1:T(8,128)(2,1)}) %all-gather.6.cloned.1.call-update) | async-done | bytes 6291472 | tf_op jit(solution)/shard_map/all_gather | solution.py:55
  123.3 9.3 %convolution_convert_fusion.1 = bf16[768,1536]{1,0:T(8,128)(2,1)} fusion(bf16[768,2048]{1,0:T(8,128)(2,1)} %all-gather.4.cloned.1.call-done, bf16[2048,1536]{0,1:T(8,128)(2,1)} %all-gather.6.cloned.1.call-done), kind=kOutput, calls=%fused_computation.6 | convolution fusion | flops 4833017856 | bytes 11796480 | tf_op jit(solution)/shard_map/dot_general | solution.py:56
  132.6 2.9 %copy.25 = bf16[768,1536]{0,1:T(8,128)(2,1)S(1)} copy(bf16[768,1536]{1,0:T(8,128)(2,1)} %convolution_convert_fusion.1) | data formatting | bytes 4718592 | tf_op jit(solution)/shard_map/convert_element_type | solution.py:61
  135.5 1.3 fusion.20
  136.8 1.5 copy.31
  138.3 1.5 copy.26
  139.8 7.6 %gather_fusion.1 = bf16[144,32,4,128]{3,1,2,0:T(8,128)(2,1)} fusion(bf16[24,32,4,128]{3,1,0,2:T(8,128)(2,1)S(1)} %bitcast.37, s32[1024]{0:T(1024)S(1)} %pad_clamp_fusion), kind=kCustom, calls=%fused_computation.1.clone | custom fusion | bytes 9437760 | tf_op jit(solution)/shard_map/jit(_take)/gather | solution.py:29
  147.4 7.6 %gather_fusion = bf16[144,32,4,128]{3,1,2,0:T(8,128)(2,1)} fusion(bf16[24,32,4,128]{3,1,0,2:T(8,128)(2,1)S(1)} %bitcast.36, s32[1024]{0:T(1024)S(1)} %pad_clamp_fusion), kind=kCustom, calls=%fused_computation.clone | custom fusion | bytes 9437760 | tf_op jit(solution)/shard_map/jit(_take)/gather | solution.py:32
  155.0 5.7 %broadcast_select_fusion = (bf16[24,6,32,4,128]{4,2,3,1,0:T(8,128)(2,1)S(1)}, bf16[24,6,32,4,128]{4,2,3,1,0:T(8,128)(2,1)}) fusion(bf16[24,6,32,4,128]{4,2,3,1,0:T(8,128)(2,1)} %bitcast.38, pred[24,6]{1,0:T(8,128)(4,1)S(1)} %copy.23, bf16[24,6,32,4,128]{4,2,3,1,0:T(8,128)(2,1)} %bitcast.39), kind=kLoop, calls=%fused_computation.3 | loop fusion | flops 4718592 | bytes 18874512 | tf_op jit(solution)/shard_map/jit(_take)/select_n | solution.py:29
  160.7 3.6 %copy.33 = bf16[24,6,32,4,128]{4,2,1,0,3:T(8,128)(2,1)} copy(bf16[24,6,32,4,128]{4,2,3,1,0:T(8,128)(2,1)S(1)} %get-tuple-element.9) | data formatting | bytes 9437184 | tf_op jit(solution)/shard_map/jit(_take)/select_n | solution.py:29
  164.2 0.4 copy.29
  164.6 5.9 %copy.28 = bf16[24,6,32,4,128]{4,2,1,3,0:T(8,128)(2,1)} copy(bf16[24,6,32,4,128]{4,2,3,1,0:T(8,128)(2,1)} %get-tuple-element.10) | data formatting | bytes 9437184 | tf_op jit(solution)/shard_map/jit(_take)/select_n | solution.py:32
  170.5 7.2 %fusion.21 = (f32[4,24,32]{2,1,0:T(8,128)S(1)}, f32[4,24,32,192]{3,2,1,0:T(8,128)}) fusion(bf16[24,32,4,128]{3,1,0,2:T(8,128)(2,1)S(1)} %bitcast.44, bf16[24,192,4,128]{3,1,0,2:T(8,128)(2,1)} %bitcast.40), kind=kOutput, calls=%fused_computation.31 | convolution fusion | flops 152764608 | bytes 7876608 | tf_op jit(solution)/shard_map/sub | solution.py:39
  177.7 5.2 %fusion.14 = bf16[24,32,4,128]{3,1,2,0:T(8,128)(2,1)S(1)} fusion(bf16[24,192,4,128]{3,1,2,0:T(8,128)(2,1)} %bitcast.43, f32[4,24,32,192]{3,2,1,0:T(8,128)} %get-tuple-element.12, f32[4,24,32]{2,1,0:T(8,128)S(1)} %get-tuple-element.11), kind=kOutput, calls=%fused_computation.22 | convolution fusion | flops 152567808 | bytes 7876608 | tf_op jit(solution)/shard_map/gqbn,qnge->qbge/dot_general | solution.py:41
  182.9 0.4 copy.35
  183.3 0.0 all-gather.8.cloned.1.call-done
  183.3 5.0 %convolution_convert_fusion = bf16[768,2048]{1,0:T(8,128)(2,1)} fusion(bf16[512,2048]{1,0:T(8,128)(2,1)} %all-gather.8.cloned.1.call-done, bf16[96,8,4,128]{3,2,1,0:T(4,128)(2,1)S(1)} %bitcast.45), kind=kOutput, calls=%fused_computation.5 | convolution fusion | flops 1612185600 | bytes 6029312 | tf_op jit(solution)/shard_map/dot_general | solution.py:66
  188.3 0.0 copy-start
  188.3 0.0 reduce-scatter.2.cloned.1.call-update
  188.4 60.6 %reduce-scatter.2.cloned.1.call-done = bf16[192,2048]{1,0:T(8,128)(2,1)} async-done(((bf16[768,2048]{1,0:T(8,128)(2,1)}), bf16[192,2048]{1,0:T(8,128)(2,1)}) %reduce-scatter.2.cloned.1.call-update) | async-done | bytes 786448 | tf_op jit(solution)/shard_map/reduce_scatter | solution.py:65
  248.9 0.0 copy-done
  248.9 1.4 fusion.7
  250.4 1.5 collective-permute-start
  251.9 17.7 %collective-permute-done = bf16[192,2048]{1,0:T(8,128)(2,1)S(1)} collective-permute-done((bf16[192,2048]{1,0:T(8,128)(2,1)S(1)}, bf16[192,2048]{1,0:T(8,128)(2,1)S(1)}, u32[]{:S(2)}, u32[]{:S(2)}) %collective-permute-start) | collective-permute-done | bytes 786464 | tf_op jit(solution)/shard_map/ppermute | solution.py:14
  269.5 0.9 copy.52
  (4 shorter events, 0.0 us)
Async XLA Ops:
  6.5 3.8 %copy-start.1 = (bf16[1,512,4,3,128]{4,2,3,1,0:T(4,128)(2,1)S(1)}, bf16[1,512,4,3,128]{4,2,3,1,0:T(4,128)(2,1)}, u32[]{:S(2)}) copy-start(bf16[1,512,4,3,128]{4,2,3,1,0:T(4,128)(2,1)} %param.9) | copy-start | bytes 4718596
  6.5 70.1 %all-gather.4.cloned.1.call-start = ((), (), s32[]{:S(2)}) async-start(), calls=%async_computation.1 | async-start | bytes 3932160 | tf_op jit(solution)/shard_map/all_gather | solution.py:57
  10.3 3.5 %copy-start.2 = (s32[1,1,24,6]{2,1,3,0:T(1,128)S(1)}, s32[1,1,24,6]{2,1,3,0:T(1,128)}, u32[]{:S(2)}) copy-start(s32[1,1,24,6]{2,1,3,0:T(1,128)} %param.11) | copy-start | bytes 1732
  10.3 113.0 %all-gather.6.cloned.1.call-start = ((), (), s32[]{:S(2)}) async-start(), calls=%async_computation.2 | async-start | bytes 7864320 | tf_op jit(solution)/shard_map/all_gather | solution.py:55
  13.0 170.3 %all-gather.8.cloned.1.call-start = ((), (), s32[]{:S(2)}) async-start(), calls=%async_computation.3 | async-start | bytes 2621440 | tf_op jit(solution)/shard_map/all_gather | solution.py:64
  13.7 235.2 %reduce-scatter.2.cloned.1.call-start = ((), (), s32[]{:S(2)}) async-start(), calls=%async_computation.4 | async-start | bytes 3932160 | tf_op jit(solution)/shard_map/reduce_scatter | solution.py:65
  188.3 60.6 %copy-start = (bf16[1,1,192,2048]{3,2,1,0:T(8,128)(2,1)S(1)}, bf16[1,1,192,2048]{3,2,1,0:T(8,128)(2,1)}, u32[]{:S(2)}) copy-start(bf16[1,1,192,2048]{3,2,1,0:T(8,128)(2,1)} %param.7) | copy-start | bytes 2359300
  250.4 19.2 %collective-permute-start = (bf16[192,2048]{1,0:T(8,128)(2,1)S(1)}, bf16[192,2048]{1,0:T(8,128)(2,1)S(1)}, u32[]{:S(2)}, u32[]{:S(2)}) collective-permute-start(bf16[192,2048]{1,0:T(8,128)(2,1)S(1)} %fusion.7), channel_id=1, source_target_pairs={{0,16},{16,0},{1,17},{17,1},{2,18},{18,2},{3,19},{19,3},{4,20},{20... | collective-permute-start | bytes 2359304 | tf_op jit(solution)/shard_map/ppermute | solution.py:14
Sparse Core Ops, SparseCore 0:
  10.5 66.1 all-gather.3
  78.2 45.0 all-gather.5
  124.9 22.5 all-gather.7
  188.5 60.4 reduce-scatter.1
where the time goes:
time: 277 us
  waiting for transfers between devices  188 us (68%)
  local copies, waits for them, and re-layouts  36.4 us (13%)
  matrix products  26.7 us (10%)
  between operations  13.2 us (5%)
  other arithmetic  10.8 us (4%)
    all_gather x1, waiting for transfers between devices, body(): lax.all_gather(normed, 'seq', axis=0, tiled=True)  62.6 us
    reduce_scatter x1, waiting for transfers between devices, body(): lax.psum_scatter(jnp.dot(mixed_rows, whole_out, preferred_element_type=jn...  60.6 us
    all_gather x1, waiting for transfers between devices, body(): whole_panel = lax.all_gather(panel_flat, 'fsdp', axis=0, tiled=True)  46.6 us
    ppermute x1, waiting for transfers between devices, passed_along(): return lax.ppermute(value, axis, pairs)  17.7 us
    dot_general x1, matrix products, body(): jnp.dot(lax.all_gather(normed, 'seq', axis=0, tiled=True), whole_panel, p...  9.27 us
    gather x1, local copies, waits for them, and re-layouts, attend(): jnp.take(value_blocks, pattern_rows, axis=0)  7.62 us
    gather x1, local copies, waits for them, and re-layouts, attend(): jnp.take(key_blocks, pattern_rows, axis=0)  7.56 us
    sub x1, matrix products, attend(): exponent = jnp.exp(scores - row_max)  7.16 us
  transfers between devices with their start and end apart: 5, of which 4 were waited for; matrix products, arithmetic and copies ran while one was open for 23% of the time, Pallas kernels for 0%

commit v1 on v0

--- a/solution.py
+++ b/solution.py
@@ -2,6 +2,7 @@
 import jax.numpy as jnp
 from jax import lax
 from jax.sharding import PartitionSpec as P
+from jax.lax import axis_index, axis_size, ppermute
 
 BLOCK = 32
 SEL = 6
@@ -45,6 +46,27 @@
 
 
 def body(arriving, gain, input_weight, output_weight, block_pattern):
+
+    def edge_bring(shard_in):
+        z2, arr_next, z = (axis_size("seq"), axis_index("seq"), shard_in.shape[0])
+        rack = tuple(((dev_j, (dev_j + 1) % z2) for dev_j in range(z2)))
+        items = tuple(((dev_j, (dev_j - 1) % z2) for dev_j in range(z2)))
+        after = jnp.zeros((*shard_in.shape[:0], z2 * z, *shard_in.shape[1:]), shard_in.dtype)
+        after = lax.dynamic_update_slice_in_dim(after, shard_in, arr_next * z, axis=0)
+        mixed_arr = carry_in = shard_in
+        block_now = z2 // 2
+        for no in [*range(1, block_now + 1)]:
+            mixed_arr = ppermute(mixed_arr, "seq", rack)
+            after = lax.dynamic_update_slice_in_dim(
+                after, mixed_arr, (arr_next - no) % z2 * z, axis=0
+            )
+            if no < z2 - block_now:
+                carry_in = ppermute(carry_in, "seq", items)
+                after = lax.dynamic_update_slice_in_dim(
+                    after, carry_in, (arr_next + no) % z2 * z, axis=0
+                )
+        return after
+
     tokens = arriving[0, 0]
     row_count = tokens.shape[0]
     normed = normalize(tokens, gain[0])
@@ -53,11 +75,7 @@
     panel_flat = input_weight[0].reshape(slab_rows, columns)
     length = row_count * lax.axis_size("seq")
     whole_panel = lax.all_gather(panel_flat, "fsdp", axis=0, tiled=True)
-    projected = jnp.dot(
-        lax.all_gather(normed, "seq", axis=0, tiled=True),
-        whole_panel,
-        preferred_element_type=jnp.float32,
-    )
+    projected = jnp.dot(edge_bring(normed), whole_panel, preferred_element_type=jnp.float32)
     projected = projected.astype(jnp.bfloat16).reshape(length, head_group, triple, head_size)
     mixed_rows = attend(projected, block_pattern[0, 0])
     out_panel = output_weight[0].reshape(head_group * head_size, -1)

time: 277 us -> 225 us (0.81)
  waiting for transfers between devices: 188 us -> 126 us
  local copies, waits for them, and re-layouts: 36.4 us -> 42.8 us
  starting transfers between devices: 1.66 us -> 6.75 us
    all_gather x1 -> x0, waiting for transfers between devices: 62.6 us -> none  [body(): lax.all_gather(normed, 'seq', axis=0, tiled=True)]
    ppermute x0 -> x3, waiting for transfers between devices: none -> 49.1 us  [the longest x2 34.8 us: edge_bring(): mixed_arr = ppermute(mixed_arr, 'seq', rack)]
    all_gather x1, waiting for transfers between devices: 46.6 us -> 0.01 us  [body(): whole_panel = lax.all_gather(panel_flat, 'fsdp', axis=0, tiled=True)]
    ppermute x0 -> x3, starting transfers between devices: none -> 5.13 us  [the longest x2 3.02 us: edge_bring(): mixed_arr = ppermute(mixed_arr, 'seq', rack)]
    dynamic_update_slice x0 -> x3, local copies, waits for them, and re-layouts: none -> 2.99 us  [the longest x2 2.05 us: edge_bring(): lax.dynamic_update_slice_in_dim(after, mixed_arr, (arr_next - no) % z2 *...]
  transfers between devices with their start and end apart: 5 -> 7, of which waited for: 4 -> 5; matrix products, arithmetic and copies ran while one was open for 23% -> 30% of each run, Pallas kernels for 0% -> 0%
where the time goes in v1:
time: 225 us
  waiting for transfers between devices  126 us (56%)
  local copies, waits for them, and re-layouts  42.8 us (19%)
  matrix products  26.6 us (12%)
  between operations  13.3 us (6%)
  other arithmetic  8.73 us (4%)
  starting transfers between devices  6.75 us (3%)
    reduce_scatter x1, waiting for transfers between devices, body(): lax.psum_scatter(jnp.dot(mixed_rows, whole_out, preferred_element_type=jn...  59.6 us
    ppermute x2, waiting for transfers between devices, edge_bring(): mixed_arr = ppermute(mixed_arr, 'seq', rack)  34.8 us
    ppermute x1, waiting for transfers between devices, passed_along(): return lax.ppermute(value, axis, pairs)  17.7 us
    ppermute x1, waiting for transfers between devices, edge_bring(): carry_in = ppermute(carry_in, 'seq', items)  14.3 us
    dot_general x1, matrix products, body(): jnp.dot(edge_bring(normed), whole_panel, preferred_element_type=jnp.float32)  9.24 us
    gather x1, local copies, waits for them, and re-layouts, attend(): jnp.take(value_blocks, pattern_rows, axis=0)  7.61 us
    gather x1, local copies, waits for them, and re-layouts, attend(): jnp.take(key_blocks, pattern_rows, axis=0)  7.57 us
    sub x1, matrix products, attend(): exponent = jnp.exp(scores - row_max)  7.15 us
  transfers between devices with their start and end apart: 7, of which 5 were waited for; matrix products, arithmetic and copies ran while one was open for 30% of the time, Pallas kernels for 0%

profile of v1, /device:TPU:0, one launch (start us, length us, event | category | flops | bytes accessed | tf_op | source)
XLA Modules:
  0.0 224.6 jit_solution(13464098414395343134)
XLA Ops:
  6.5 0.0 copy-start
  6.5 0.0 all-gather.3.cloned.1.call-start
  6.5 3.8 %copy.24 = bf16[1,512,4,3,128]{1,4,3,2,0:T(8,128)(2,1)} copy(bf16[1,512,4,3,128]{4,2,3,1,0:T(4,128)(2,1)} %param.9) | data formatting | bytes 3145728 | tf_op args[2]
  10.4 0.0 all-gather.3.cloned.1.call-update
  10.4 0.0 all-gather.5.cloned.1.call-start
  10.5 0.0 copy-done
  10.5 0.2 fusion.4
  10.7 2.1 broadcast_in_dim.18
  12.8 0.0 copy-done.3
  12.8 1.4 constant_dynamic-update-slice_fusion.3
  14.2 3.0 %collective-permute-start = (bf16[192,2048]{1,0:T(8,128)(2,1)}, bf16[192,2048]{1,0:T(8,128)(2,1)S(1)}, u32[]{:S(2)}, u32[]{:S(2)}) collective-permute-start(bf16[192,2048]{1,0:T(8,128)(2,1)} %get-tuple-element.7), channel_id=1, source_target_pairs={{0,1},{1,2},{2,3},{3,0},{4,5},{5,6},{6,7},{7,4},{8,9},{9,10},{10,1... | collective-permute-start | bytes 2359304 | tf_op jit(solution)/shard_map/ppermute | solution.py:59
  17.2 2.1 collective-permute-start.1
  19.3 0.0 all-gather.5.cloned.1.call-update
  19.4 0.0 reduce-scatter.2.cloned.1.call-start
  19.5 0.0 copy-done.2
  19.5 0.1 copy.27
  19.6 0.1 reshape.54
  19.7 18.3 %collective-permute-done = bf16[192,2048]{1,0:T(8,128)(2,1)S(1)} collective-permute-done((bf16[192,2048]{1,0:T(8,128)(2,1)}, bf16[192,2048]{1,0:T(8,128)(2,1)S(1)}, u32[]{:S(2)}, u32[]{:S(2)}) %collective-permute-start) | collective-permute-done | bytes 786464 | tf_op jit(solution)/shard_map/ppermute | solution.py:59
  38.0 0.0 collective-permute-start.2
  38.0 0.1 copy.23
  38.1 1.0 constant_dynamic-update-slice_fusion.2
  39.1 14.3 %collective-permute-done.1 = bf16[192,2048]{1,0:T(8,128)(2,1)S(1)} collective-permute-done((bf16[192,2048]{1,0:T(8,128)(2,1)}, bf16[192,2048]{1,0:T(8,128)(2,1)S(1)}, u32[]{:S(2)}, u32[]{:S(2)}) %collective-permute-start.1) | collective-permute-done | bytes 786464 | tf_op jit(solution)/shard_map/ppermute | solution.py:64
  53.4 0.9 constant_dynamic-update-slice_fusion.1
  54.4 16.5 %collective-permute-done.2 = bf16[192,2048]{1,0:T(8,128)(2,1)S(1)} collective-permute-done((bf16[192,2048]{1,0:T(8,128)(2,1)S(1)}, bf16[192,2048]{1,0:T(8,128)(2,1)S(1)}, u32[]{:S(2)}, u32[]{:S(2)}) %collective-permute-start.2) | collective-permute-done | bytes 786464 | tf_op jit(solution)/shard_map/ppermute | solution.py:59
  70.8 1.0 constant_dynamic-update-slice_fusion
  71.9 9.2 %convolution_convert_fusion.1 = bf16[768,1536]{1,0:T(8,128)(2,1)} fusion(bf16[768,2048]{1,0:T(8,128)(2,1)} %constant_dynamic-update-slice_fusion, bf16[2048,1536]{0,1:T(8,128)(2,1)} %all-gather.3.cloned.1.call-done), kind=kOutput, calls=%fused_computation.6 | convolution fusion | flops 4833017856 | bytes 11796480 | tf_op jit(solution)/shard_map/dot_general | solution.py:78
  81.1 2.9 %copy.25 = bf16[768,1536]{0,1:T(8,128)(2,1)S(1)} copy(bf16[768,1536]{1,0:T(8,128)(2,1)} %convolution_convert_fusion.1) | data formatting | bytes 4718592 | tf_op jit(solution)/shard_map/convert_element_type | solution.py:79
  84.0 1.5 fusion.21
  85.4 1.5 copy.31
  86.9 1.5 copy.26
  88.4 7.6 %gather_fusion.1 = bf16[144,32,4,128]{3,1,2,0:T(8,128)(2,1)} fusion(bf16[24,32,4,128]{3,1,0,2:T(8,128)(2,1)S(1)} %bitcast.38, s32[1024]{0:T(1024)S(1)} %pad_clamp_fusion), kind=kCustom, calls=%fused_computation.1.clone | custom fusion | bytes 9437760 | tf_op jit(solution)/shard_map/jit(_take)/gather | solution.py:30
  96.0 7.6 %gather_fusion = bf16[144,32,4,128]{3,1,2,0:T(8,128)(2,1)} fusion(bf16[24,32,4,128]{3,1,0,2:T(8,128)(2,1)S(1)} %bitcast.37, s32[1024]{0:T(1024)S(1)} %pad_clamp_fusion), kind=kCustom, calls=%fused_computation.clone | custom fusion | bytes 9437760 | tf_op jit(solution)/shard_map/jit(_take)/gather | solution.py:33
  103.6 5.7 %broadcast_select_fusion = (bf16[24,6,32,4,128]{4,2,3,1,0:T(8,128)(2,1)S(1)}, bf16[24,6,32,4,128]{4,2,3,1,0:T(8,128)(2,1)}) fusion(bf16[24,6,32,4,128]{4,2,3,1,0:T(8,128)(2,1)} %bitcast.39, pred[24,6]{1,0:T(8,128)(4,1)S(1)} %copy.23, bf16[24,6,32,4,128]{4,2,3,1,0:T(8,128)(2,1)} %bitcast.40), kind=kLoop, calls=%fused_computation.3 | loop fusion | flops 4718592 | bytes 18874512 | tf_op jit(solution)/shard_map/jit(_take)/select_n | solution.py:30
  109.3 3.5 %copy.33 = bf16[24,6,32,4,128]{4,2,1,0,3:T(8,128)(2,1)} copy(bf16[24,6,32,4,128]{4,2,3,1,0:T(8,128)(2,1)S(1)} %get-tuple-element.11) | data formatting | bytes 9437184 | tf_op jit(solution)/shard_map/jit(_take)/select_n | solution.py:30
  112.8 0.0 copy-done.1
  112.8 0.4 copy.29
  113.2 6.0 %copy.28 = bf16[24,6,32,4,128]{4,2,1,3,0:T(8,128)(2,1)} copy(bf16[24,6,32,4,128]{4,2,3,1,0:T(8,128)(2,1)} %get-tuple-element.12) | data formatting | bytes 9437184 | tf_op jit(solution)/shard_map/jit(_take)/select_n | solution.py:33
  119.1 7.2 %fusion.22 = (f32[4,24,32]{2,1,0:T(8,128)S(1)}, f32[4,24,32,192]{3,2,1,0:T(8,128)}) fusion(bf16[24,32,4,128]{3,1,0,2:T(8,128)(2,1)S(1)} %bitcast.45, bf16[24,192,4,128]{3,1,0,2:T(8,128)(2,1)} %bitcast.41), kind=kOutput, calls=%fused_computation.35 | convolution fusion | flops 152764608 | bytes 7876608 | tf_op jit(solution)/shard_map/sub | solution.py:40
  126.3 5.2 %fusion.14 = bf16[24,32,4,128]{3,1,2,0:T(8,128)(2,1)S(1)} fusion(bf16[24,192,4,128]{3,1,2,0:T(8,128)(2,1)} %bitcast.44, f32[4,24,32,192]{3,2,1,0:T(8,128)} %get-tuple-element.14, f32[4,24,32]{2,1,0:T(8,128)S(1)} %get-tuple-element.13), kind=kOutput, calls=%fused_computation.22 | convolution fusion | flops 152567808 | bytes 7876608 | tf_op jit(solution)/shard_map/gqbn,qnge->qbge/dot_general | solution.py:42
  131.5 0.4 copy.35
  131.9 0.0 all-gather.5.cloned.1.call-done
  131.9 5.0 %convolution_convert_fusion = bf16[768,2048]{1,0:T(8,128)(2,1)} fusion(bf16[512,2048]{1,0:T(8,128)(2,1)} %all-gather.5.cloned.1.call-done, bf16[96,8,4,128]{3,2,1,0:T(4,128)(2,1)S(1)} %bitcast.46), kind=kOutput, calls=%fused_computation.5 | convolution fusion | flops 1612185600 | bytes 6029312 | tf_op jit(solution)/shard_map/dot_general | solution.py:84
  137.0 0.0 reduce-scatter.2.cloned.1.call-update
  137.0 59.6 %reduce-scatter.2.cloned.1.call-done = bf16[192,2048]{1,0:T(8,128)(2,1)} async-done(((bf16[768,2048]{1,0:T(8,128)(2,1)}), bf16[192,2048]{1,0:T(8,128)(2,1)}) %reduce-scatter.2.cloned.1.call-update) | async-done | bytes 786448 | tf_op jit(solution)/shard_map/reduce_scatter | solution.py:83
  196.6 1.4 fusion.7
  198.0 1.5 collective-permute-start.3
  199.5 17.7 %collective-permute-done.3 = bf16[192,2048]{1,0:T(8,128)(2,1)S(1)} collective-permute-done((bf16[192,2048]{1,0:T(8,128)(2,1)S(1)}, bf16[192,2048]{1,0:T(8,128)(2,1)S(1)}, u32[]{:S(2)}, u32[]{:S(2)}) %collective-permute-start.3) | collective-permute-done | bytes 786464 | tf_op jit(solution)/shard_map/ppermute | solution.py:15
  217.2 0.9 copy.56
  (8 shorter events, 0.0 us)
Async XLA Ops:
  6.5 3.9 %copy-start = (bf16[1,1,192,2048]{3,2,1,0:T(8,128)(2,1)S(1)}, bf16[1,1,192,2048]{3,2,1,0:T(8,128)(2,1)}, u32[]{:S(2)}) copy-start(bf16[1,1,192,2048]{3,2,1,0:T(8,128)(2,1)} %param.7) | copy-start | bytes 2359300
  6.5 65.3 %all-gather.3.cloned.1.call-start = ((), (), s32[]{:S(2)}) async-start(), calls=%async_computation.1 | async-start | bytes 7864320 | tf_op jit(solution)/shard_map/all_gather | solution.py:77
  10.4 2.4 %copy-start.3 = (f32[1,2048]{1,0:T(1,128)S(1)}, f32[1,2048]{1,0:T(1,128)}, u32[]{:S(2)}) copy-start(f32[1,2048]{1,0:T(1,128)} %param.8) | copy-start | bytes 24580
  10.4 121.5 %all-gather.5.cloned.1.call-start = ((), (), s32[]{:S(2)}) async-start(), calls=%async_computation.2 | async-start | bytes 2621440 | tf_op jit(solution)/shard_map/all_gather | solution.py:82
  10.7 8.8 %copy-start.2 = (s32[1,1,24,6]{2,1,3,0:T(1,128)S(1)}, s32[1,1,24,6]{2,1,3,0:T(1,128)}, u32[]{:S(2)}) copy-start(s32[1,1,24,6]{2,1,3,0:T(1,128)} %param.11) | copy-start | bytes 1732
  14.2 23.8 %collective-permute-start = (bf16[192,2048]{1,0:T(8,128)(2,1)}, bf16[192,2048]{1,0:T(8,128)(2,1)S(1)}, u32[]{:S(2)}, u32[]{:S(2)}) collective-permute-start(bf16[192,2048]{1,0:T(8,128)(2,1)} %get-tuple-element.7), channel_id=1, source_target_pairs={{0,1},{1,2},{2,3},{3,0},{4,5},{5,6},{6,7},{7,4},{8,9},{9,10},{10,1... | collective-permute-start | bytes 2359304 | tf_op jit(solution)/shard_map/ppermute | solution.py:59
  17.2 36.2 %collective-permute-start.1 = (bf16[192,2048]{1,0:T(8,128)(2,1)}, bf16[192,2048]{1,0:T(8,128)(2,1)S(1)}, u32[]{:S(2)}, u32[]{:S(2)}) collective-permute-start(bf16[192,2048]{1,0:T(8,128)(2,1)} %get-tuple-element.7), channel_id=1, source_target_pairs={{0,3},{1,0},{2,1},{3,2},{4,7},{5,4},{6,5},{7,6},{8,11},{9,8},{10,9... | collective-permute-start | bytes 2359304 | tf_op jit(solution)/shard_map/ppermute | solution.py:64
  19.4 177.2 %reduce-scatter.2.cloned.1.call-start = ((), (), s32[]{:S(2)}) async-start(), calls=%async_computation.3 | async-start | bytes 3932160 | tf_op jit(solution)/shard_map/reduce_scatter | solution.py:83
  38.0 32.9 %collective-permute-start.2 = (bf16[192,2048]{1,0:T(8,128)(2,1)S(1)}, bf16[192,2048]{1,0:T(8,128)(2,1)S(1)}, u32[]{:S(2)}, u32[]{:S(2)}) collective-permute-start(bf16[192,2048]{1,0:T(8,128)(2,1)S(1)} %collective-permute-done), channel_id=1, source_target_pairs={{0,1},{1,2},{2,3},{3,0},{4,5},{5,6},{6,7},{7,4},{8,9},{9,10},{10,1... | collective-permute-start | bytes 2359304 | tf_op jit(solution)/shard_map/ppermute | solution.py:59
  109.3 3.5 %copy-start.1 = (bf16[768,4,1,128]{0,3,2,1:T(8,128)(2,1)S(1)}, bf16[768,4,1,128]{0,3,2,1:T(8,128)(2,1)}, u32[]{:S(2)}) copy-start(bf16[768,4,1,128]{0,3,2,1:T(8,128)(2,1)} %get-tuple-element.9) | copy-start | bytes 2359300
  198.0 19.2 %collective-permute-start.3 = (bf16[192,2048]{1,0:T(8,128)(2,1)S(1)}, bf16[192,2048]{1,0:T(8,128)(2,1)S(1)}, u32[]{:S(2)}, u32[]{:S(2)}) collective-permute-start(bf16[192,2048]{1,0:T(8,128)(2,1)S(1)} %fusion.7), channel_id=1, source_target_pairs={{0,16},{16,0},{1,17},{17,1},{2,18},{18,2},{3,19},{19,3},{4,20},{20... | collective-permute-start | bytes 2359304 | tf_op jit(solution)/shard_map/ppermute | solution.py:15
Sparse Core Ops, SparseCore 0:
  10.5 49.0 all-gather.2
  61.2 22.5 all-gather.4
  137.1 59.4 reduce-scatter.1
